TPU v7x, 32 devices: a whole 2x2x4 slice. The times are simulated.
32 devices in a mesh: groups: 2 (over y), frame: 4 (over z), space: 4 (over x, core).
Axes of the slice: x: 2, y: 2, z: 4, core: 2. Of those that a mesh axis runs over, the one named last changes fastest.
Arguments:
- queries: float32 [16384, 128], P(('groups', 'frame', 'space')), parts along dimension 0, may hold values from -256 to 256
- keys: float32 [16384, 128], P(('groups', 'frame', 'space')), parts along dimension 0, may hold values from -8 to 8
- values: float32 [16384, 128], P(('groups', 'frame', 'space')), parts along dimension 0, may hold values from -6 to 6
- block_mask: int32 [4, 4], replicated, may hold values from 0 to 1, as said below
- partner_flags: int32 [4, 2, 2], replicated, may hold values 0 or 1
Outputs:
- attended: float32 [16384, 128], P(('groups', 'frame', 'space')), parts along dimension 0
There are 2 independent parts, one for each index of `groups`. A program takes and returns all parts, laid end to end along the dimension named above; an argument that names none is the same for every part. Nothing has to cross between parts.
Inputs may be any that keep to these rules, and one draw needn't show every extreme that they name: block_mask[a, b] = 1 when a = b or |a - b| = 2, and block_mask[a, b] = 0 when |a - b| > 2. `partner_flags`: a partner outside frame groups 0 to 3 is never used, whatever its flag.
All inputs are finite; a program needn't handle non-finite values.
Results may differ from a plain program's by a relative error of at most 0.0003.
Values sent between devices are 32-bit elements; how exact they have to be, the bound alone decides.
A program may use at most 64 MiB of HBM per device.

v0:
```python
import math

import jax
import jax.numpy as jnp
from jax import lax
from jax.sharding import PartitionSpec as P

masked_score = -1e30


def shifted(block, axis, distance):
    devices = range(lax.axis_size(axis))
    route = [(i - distance, i) for i in devices if i - distance in devices]
    return lax.ppermute(block, axis, route)


def score_block(query_rows, key_rows):
    return lax.dot_general(
        query_rows,
        key_rows,
        (((1,), (1,)), ((), ())),
        precision=lax.Precision.HIGHEST,
        preferred_element_type=jnp.float32,
    )


def absorb(state, query_rows, key_rows, value_rows, allowed):
    row_count, head_width = key_rows.shape
    block_rows = 512
    block_count = row_count // block_rows
    score_scale = 1.0 / math.sqrt(head_width)

    def absorb_block(carried, pieces):
        key_block, value_block, allowed_block = pieces
        running_max, row_total, weighted = carried
        scores = score_block(query_rows, key_block) * score_scale
        scores = jnp.where(allowed_block[None, :], scores, masked_score)
        new_max = jnp.maximum(running_max, jnp.max(scores, axis=1))
        weights = jnp.where(allowed_block[None, :], jnp.exp(scores - new_max[:, None]), 0.0)
        factor = jnp.exp(running_max - new_max)
        row_total = row_total * factor + jnp.sum(weights, axis=1)
        weighted = weighted * factor[:, None] + jnp.dot(
            weights,
            value_block,
            precision=lax.Precision.HIGHEST,
            preferred_element_type=jnp.float32,
        )
        return ((new_max, row_total, weighted), None)

    carried, _ = lax.scan(
        absorb_block,
        state,
        (
            key_rows.reshape(block_count, block_rows, head_width),
            value_rows.reshape(block_count, block_rows, head_width),
            allowed.reshape(block_count, block_rows),
        ),
    )
    return carried


def per_device(queries, keys, values, block_mask, partner_flags):
    tok_rows, head_width = queries.shape
    blocks = lax.axis_size("space")
    groups = lax.axis_size("frame")
    levels = groups.bit_length() - 1
    space_index = lax.axis_index("space")
    group_index = lax.axis_index("frame")
    own_row = lax.dynamic_index_in_dim(block_mask, space_index, 0, keepdims=False)
    flag_rows = lax.dynamic_index_in_dim(partner_flags, group_index, 0, keepdims=False)
    far_keys = []
    far_values = []
    far_allowed = []
    for level_index in range(levels):
        distance = 2**level_index
        for direction in range(2):
            offset = distance if direction == 0 else -distance
            moved_keys, moved_values = shifted((keys, values), "frame", offset)
            partner = group_index - offset
            usable = (partner >= 0) & (partner < groups) & (flag_rows[level_index, direction] > 0)
            far_keys.append(moved_keys)
            far_values.append(moved_values)
            far_allowed.append(jnp.broadcast_to(usable, (tok_rows,)))
    initial = (
        jnp.full((tok_rows,), masked_score, jnp.float32),
        jnp.zeros((tok_rows,), jnp.float32),
        jnp.zeros((tok_rows, head_width), jnp.float32),
    )
    state = absorb(
        initial,
        queries,
        jnp.concatenate(far_keys, axis=0),
        jnp.concatenate(far_values, axis=0),
        jnp.concatenate(far_allowed, axis=0),
    )
    key_piece = lax.all_gather(keys, "space", axis=0, tiled=True)
    value_piece = lax.all_gather(values, "space", axis=0, tiled=True)
    row_count = key_piece.shape[0]
    owner = lax.broadcasted_iota(jnp.int32, (row_count,), 0) // tok_rows
    matched = owner[:, None] == lax.broadcasted_iota(jnp.int32, (1, blocks), 1)
    allowed = jnp.any(matched & (own_row[None, :] > 0), axis=1)
    state = absorb(state, queries, key_piece, value_piece, allowed)
    running_max, row_total, weighted = state
    return weighted / row_total[:, None]


def solution(mesh):
    in_specs = (
        P(("groups", "frame", "space"), None),
        P(("groups", "frame", "space"), None),
        P(("groups", "frame", "space"), None),
        P(),
        P(),
    )
    out_specs = P(("groups", "frame", "space"), None)
    return jax.shard_map(
        per_device, mesh=mesh, in_specs=in_specs, out_specs=out_specs, check_vma=False
    )
```

profile of v0, /device:TPU:0, one launch (start us, length us, event | category | flops | bytes accessed | tf_op | source)
XLA Modules:
  0.0 99.5 jit_solution(3641384196366600638)
XLA Ops:
  6.5 0.7 all-gather.5.cloned.1.call-update
  7.3 0.0 all-gather.3.cloned.1.call-start
  7.3 4.9 %collective-permute-start = (f32[512,128]{1,0:T(8,128)}, f32[512,128]{1,0:T(8,128)S(1)}, u32[]{:S(2)}, u32[]{:S(2)}) collective-permute-start(f32[512,128]{1,0:T(8,128)} %param.10), channel_id=1, source_target_pairs={{0,4},{4,8},{8,12},{1,5},{5,9},{9,13},{2,6},{6,10},{10,14},{3,7},{... | collective-permute-start | bytes 786440 | tf_op jit(solution)/shard_map/ppermute | solution.py:14
  12.3 1.3 %collective-permute-start.1 = (f32[512,128]{1,0:T(8,128)}, f32[512,128]{1,0:T(8,128)S(1)}, u32[]{:S(2)}, u32[]{:S(2)}) collective-permute-start(f32[512,128]{1,0:T(8,128)} %param.10), channel_id=1, source_target_pairs={{4,0},{8,4},{12,8},{5,1},{9,5},{13,9},{6,2},{10,6},{14,10},{7,3},{... | collective-permute-start | bytes 786440 | tf_op jit(solution)/shard_map/ppermute | solution.py:14
  13.6 5.6 %collective-permute-start.2 = (f32[512,128]{1,0:T(8,128)}, f32[512,128]{1,0:T(8,128)S(1)}, u32[]{:S(2)}, u32[]{:S(2)}) collective-permute-start(f32[512,128]{1,0:T(8,128)} %param.10), channel_id=1, source_target_pairs={{0,8},{4,12},{1,9},{5,13},{2,10},{6,14},{3,11},{7,15},{16,24},{20,... | collective-permute-start | bytes 786440 | tf_op jit(solution)/shard_map/ppermute | solution.py:14
  19.1 1.3 %collective-permute-start.3 = (f32[512,128]{1,0:T(8,128)}, f32[512,128]{1,0:T(8,128)S(1)}, u32[]{:S(2)}, u32[]{:S(2)}) collective-permute-start(f32[512,128]{1,0:T(8,128)} %param.10), channel_id=1, source_target_pairs={{8,0},{12,4},{9,1},{13,5},{10,2},{14,6},{11,3},{15,7},{24,16},{28,... | collective-permute-start | bytes 786440 | tf_op jit(solution)/shard_map/ppermute | solution.py:14
  20.4 3.5 %collective-permute-start.4 = (f32[512,128]{1,0:T(8,128)S(1)}, f32[512,128]{1,0:T(8,128)S(1)}, u32[]{:S(2)}, u32[]{:S(2)}) collective-permute-start(f32[512,128]{1,0:T(8,128)S(1)} %copy-done.2), channel_id=1, source_target_pairs={{0,4},{4,8},{8,12},{1,5},{5,9},{9,13},{2,6},{6,10},{10,14},{3,7},{... | collective-permute-start | bytes 786440 | tf_op jit(solution)/shard_map/ppermute | solution.py:14
  24.0 0.0 all-gather.3.cloned.1.call-update
  24.0 0.2 dynamic-slice_reduce_fusion.2
  24.2 0.6 fusion.32
  24.8 0.7 compare_bitcast_fusion
  27.9 0.1 fusion.26
  28.1 1.3 %collective-permute-start.5 = (f32[512,128]{1,0:T(8,128)S(1)}, f32[512,128]{1,0:T(8,128)S(1)}, u32[]{:S(2)}, u32[]{:S(2)}) collective-permute-start(f32[512,128]{1,0:T(8,128)S(1)} %copy-done.2), channel_id=1, source_target_pairs={{4,0},{8,4},{12,8},{5,1},{9,5},{13,9},{6,2},{10,6},{14,10},{7,3},{... | collective-permute-start | bytes 786440 | tf_op jit(solution)/shard_map/ppermute | solution.py:14
  29.4 6.5 %collective-permute-start.6 = (f32[512,128]{1,0:T(8,128)S(1)}, f32[512,128]{1,0:T(8,128)S(1)}, u32[]{:S(2)}, u32[]{:S(2)}) collective-permute-start(f32[512,128]{1,0:T(8,128)S(1)} %copy-done.2), channel_id=1, source_target_pairs={{0,8},{4,12},{1,9},{5,13},{2,10},{6,14},{3,11},{7,15},{16,24},{20,... | collective-permute-start | bytes 786440 | tf_op jit(solution)/shard_map/ppermute | solution.py:14
  35.9 1.3 %collective-permute-start.7 = (f32[512,128]{1,0:T(8,128)S(1)}, f32[512,128]{1,0:T(8,128)}, u32[]{:S(2)}, u32[]{:S(2)}) collective-permute-start(f32[512,128]{1,0:T(8,128)S(1)} %copy-done.2), channel_id=1, source_target_pairs={{8,0},{12,4},{9,1},{13,5},{10,2},{14,6},{11,3},{15,7},{24,16},{28,... | collective-permute-start | bytes 786440 | tf_op jit(solution)/shard_map/ppermute | solution.py:14
  37.3 0.1 pad_maximum_fusion
  37.4 3.6 %collective-permute-done.5 = f32[512,128]{1,0:T(8,128)S(1)} collective-permute-done((f32[512,128]{1,0:T(8,128)S(1)}, f32[512,128]{1,0:T(8,128)S(1)}, u32[]{:S(2)}, u32[]{:S(2)}) %collective-permute-start.5) | collective-permute-done | bytes 262176 | tf_op jit(solution)/shard_map/ppermute | solution.py:14
  41.0 10.9 %collective-permute-done.7 = f32[512,128]{1,0:T(8,128)} collective-permute-done((f32[512,128]{1,0:T(8,128)S(1)}, f32[512,128]{1,0:T(8,128)}, u32[]{:S(2)}, u32[]{:S(2)}) %collective-permute-start.7) | collective-permute-done | bytes 262176 | tf_op jit(solution)/shard_map/ppermute | solution.py:14
  52.0 2.0 %pad_maximum_fusion.1 = f32[2048,128]{1,0:T(8,128)} fusion(f32[512,128]{1,0:T(8,128)} %collective-permute-done.7, f32[512,128]{1,0:T(8,128)S(1)} %collective-permute-done.6, f32[512,128]{1,0:T(8,128)S(1)} %collective-permute-done.5, f32[512,128]{1,0:T(8,128)S(1)} %collective-permute-done.4), kind=kLoop, calls=%fused_computation.40 | loop fusion | flops 786432 | bytes 2097152 | tf_op jit(solution)/shard_map/concatenate | solution.py:93
  54.0 17.0 %while.30 = (s32[]{:T(128)}, f32[512]{0:T(512)S(1)}, f32[512]{0:T(512)S(1)}, f32[512,128]{1,0:T(8,128)S(1)}, pred[4,512]{1,0:T(4,128)(4,1)S(1)}, /*index=5*/f32[...) while((s32[]{:T(128)}, f32[512]{0:T(512)S(1)}, ...), condition=%wide.region_3.4_spmd.clone, body=%wide.region_0.3_spmd.clone.sunk | while | flops 807602688 | bytes 4492409 | solution.py:50
  54.0 1.0 %fusion.50 = (f32[512]{0:T(512)S(1)}, f32[512,512]{1,0:T(8,128)S(1)}) fusion(f32[512,128]{1,0:T(8,128)S(1)} %get-tuple-element.308, f32[4,512,128]{2,1,0:T(8,128)S(1)} %get-tuple-element.307, s32[]{:T(128)} %get-tuple-element.292, pred[512]{0:T(512)(128)(4,1)S(1)} %dynamic-slice_reduce_fusion.6), kind=kOutput, calls=%fused_computation.56.clone.1 | convolution fusion | flops 403439104 | bytes 1575428 | tf_op jit(solution)/shard_map/while/body/eval_jaxpr/dot_general | solution.py:18
  55.1 0.2 fusion.51
  55.3 2.9 %convolution_add_fusion.5 = f32[512,128]{1,0:T(8,128)S(1)} fusion(f32[512,512]{1,0:T(8,128)S(1)} %get-tuple-element.279, f32[512]{0:T(512)S(1)} %select_maximum_fusion.2, pred[512]{0:T(512)(128)(4,1)S(1)} %dynamic-slice_reduce_fusion.6, f32[512,128]{1,0:T(8,128)S(1)} %get-tuple-element.295, f32[4,512,128]{2,1,0:T(8,128)} %get-tuple-element.309, ...), kind=kOutput, calls=%fused_computation.20.clone.1 | convolution fusion | flops 403374080 | bytes 1840129 | tf_op jit(solution)/shard_map/while/body/eval_jaxpr/dot_general | solution.py:42
  58.3 1.0 %fusion.50 = (f32[512]{0:T(512)S(1)}, f32[512,512]{1,0:T(8,128)S(1)}) fusion(f32[512,128]{1,0:T(8,128)S(1)} %get-tuple-element.308, f32[4,512,128]{2,1,0:T(8,128)S(1)} %get-tuple-element.307, s32[]{:T(128)} %get-tuple-element.292, pred[512]{0:T(512)(128)(4,1)S(1)} %dynamic-slice_reduce_fusion.6), kind=kOutput, calls=%fused_computation.56.clone.1 | convolution fusion | flops 403439104 | bytes 1575428 | tf_op jit(solution)/shard_map/while/body/eval_jaxpr/dot_general | solution.py:18
  59.3 0.2 fusion.51
  59.6 2.9 %convolution_add_fusion.5 = f32[512,128]{1,0:T(8,128)S(1)} fusion(f32[512,512]{1,0:T(8,128)S(1)} %get-tuple-element.279, f32[512]{0:T(512)S(1)} %select_maximum_fusion.2, pred[512]{0:T(512)(128)(4,1)S(1)} %dynamic-slice_reduce_fusion.6, f32[512,128]{1,0:T(8,128)S(1)} %get-tuple-element.295, f32[4,512,128]{2,1,0:T(8,128)} %get-tuple-element.309, ...), kind=kOutput, calls=%fused_computation.20.clone.1 | convolution fusion | flops 403374080 | bytes 1840129 | tf_op jit(solution)/shard_map/while/body/eval_jaxpr/dot_general | solution.py:42
  62.5 1.1 %fusion.50 = (f32[512]{0:T(512)S(1)}, f32[512,512]{1,0:T(8,128)S(1)}) fusion(f32[512,128]{1,0:T(8,128)S(1)} %get-tuple-element.308, f32[4,512,128]{2,1,0:T(8,128)S(1)} %get-tuple-element.307, s32[]{:T(128)} %get-tuple-element.292, pred[512]{0:T(512)(128)(4,1)S(1)} %dynamic-slice_reduce_fusion.6), kind=kOutput, calls=%fused_computation.56.clone.1 | convolution fusion | flops 403439104 | bytes 1575428 | tf_op jit(solution)/shard_map/while/body/eval_jaxpr/dot_general | solution.py:18
  63.6 0.2 fusion.51
  63.8 2.9 %convolution_add_fusion.5 = f32[512,128]{1,0:T(8,128)S(1)} fusion(f32[512,512]{1,0:T(8,128)S(1)} %get-tuple-element.279, f32[512]{0:T(512)S(1)} %select_maximum_fusion.2, pred[512]{0:T(512)(128)(4,1)S(1)} %dynamic-slice_reduce_fusion.6, f32[512,128]{1,0:T(8,128)S(1)} %get-tuple-element.295, f32[4,512,128]{2,1,0:T(8,128)} %get-tuple-element.309, ...), kind=kOutput, calls=%fused_computation.20.clone.1 | convolution fusion | flops 403374080 | bytes 1840129 | tf_op jit(solution)/shard_map/while/body/eval_jaxpr/dot_general | solution.py:42
  66.8 1.1 %fusion.50 = (f32[512]{0:T(512)S(1)}, f32[512,512]{1,0:T(8,128)S(1)}) fusion(f32[512,128]{1,0:T(8,128)S(1)} %get-tuple-element.308, f32[4,512,128]{2,1,0:T(8,128)S(1)} %get-tuple-element.307, s32[]{:T(128)} %get-tuple-element.292, pred[512]{0:T(512)(128)(4,1)S(1)} %dynamic-slice_reduce_fusion.6), kind=kOutput, calls=%fused_computation.56.clone.1 | convolution fusion | flops 403439104 | bytes 1575428 | tf_op jit(solution)/shard_map/while/body/eval_jaxpr/dot_general | solution.py:18
  67.8 0.2 fusion.51
  68.1 2.9 %convolution_add_fusion.5 = f32[512,128]{1,0:T(8,128)S(1)} fusion(f32[512,512]{1,0:T(8,128)S(1)} %get-tuple-element.279, f32[512]{0:T(512)S(1)} %select_maximum_fusion.2, pred[512]{0:T(512)(128)(4,1)S(1)} %dynamic-slice_reduce_fusion.6, f32[512,128]{1,0:T(8,128)S(1)} %get-tuple-element.295, f32[4,512,128]{2,1,0:T(8,128)} %get-tuple-element.309, ...), kind=kOutput, calls=%fused_computation.20.clone.1 | convolution fusion | flops 403374080 | bytes 1840129 | tf_op jit(solution)/shard_map/while/body/eval_jaxpr/dot_general | solution.py:42
  71.0 0.0 all-gather.5.cloned.1.call-done
  71.0 0.0 all-gather.3.cloned.1.call-done
  71.1 20.8 %while.29 = (s32[]{:T(128)}, f32[512]{0:T(512)S(1)}, f32[512]{0:T(512)S(1)}, f32[512,128]{1,0:T(8,128)S(1)}, pred[4,512]{1,0:T(4,128)(4,1)S(1)}, /*index=5*/f32[...) while((s32[]{:T(128)}, f32[512]{0:T(512)S(1)}, f32[512]{0:T(512)S(1)}, ...), condition=%wide.region_8.9_spmd, body=%wide.region_5.8_spmd.sunk | while | flops 807535616 | bytes 4492897 | solution.py:50
  71.1 2.0 %fusion.46 = (f32[512]{0:T(512)S(1)}, f32[512,512]{1,0:T(8,128)S(1)}) fusion(f32[512,128]{1,0:T(8,128)S(1)} %get-tuple-element.336, f32[4,512,128]{2,1,0:T(8,128)} %get-tuple-element.335, s32[]{:T(128)} %get-tuple-element.321, pred[512]{0:T(512)(128)(4,1)S(1)} %dynamic-slice_reduce_fusion.5), kind=kOutput, calls=%fused_computation.55.clone.1 | convolution fusion | flops 403439104 | bytes 1575936 | tf_op jit(solution)/shard_map/while/body/eval_jaxpr/dot_general | solution.py:18
  73.1 0.2 fusion.47
  73.3 2.9 %convolution_add_fusion.4 = f32[512,128]{1,0:T(8,128)S(1)} fusion(f32[512,512]{1,0:T(8,128)S(1)} %get-tuple-element.267, f32[512]{0:T(512)S(1)} %max.10, pred[512]{0:T(512)(128)(4,1)S(1)} %dynamic-slice_reduce_fusion.5, f32[4,512,128]{2,1,0:T(8,128)} %get-tuple-element.337, s32[]{:T(128)} %get-tuple-element.321, ...), kind=kOutput, calls=%fused_computation.2.clone.1 | convolution fusion | flops 403308544 | bytes 1840128 | tf_op jit(solution)/shard_map/while/body/eval_jaxpr/dot_general | solution.py:42
  76.3 2.0 %fusion.46 = (f32[512]{0:T(512)S(1)}, f32[512,512]{1,0:T(8,128)S(1)}) fusion(f32[512,128]{1,0:T(8,128)S(1)} %get-tuple-element.336, f32[4,512,128]{2,1,0:T(8,128)} %get-tuple-element.335, s32[]{:T(128)} %get-tuple-element.321, pred[512]{0:T(512)(128)(4,1)S(1)} %dynamic-slice_reduce_fusion.5), kind=kOutput, calls=%fused_computation.55.clone.1 | convolution fusion | flops 403439104 | bytes 1575936 | tf_op jit(solution)/shard_map/while/body/eval_jaxpr/dot_general | solution.py:18
  78.3 0.2 fusion.47
  78.5 2.9 %convolution_add_fusion.4 = f32[512,128]{1,0:T(8,128)S(1)} fusion(f32[512,512]{1,0:T(8,128)S(1)} %get-tuple-element.267, f32[512]{0:T(512)S(1)} %max.10, pred[512]{0:T(512)(128)(4,1)S(1)} %dynamic-slice_reduce_fusion.5, f32[4,512,128]{2,1,0:T(8,128)} %get-tuple-element.337, s32[]{:T(128)} %get-tuple-element.321, ...), kind=kOutput, calls=%fused_computation.2.clone.1 | convolution fusion | flops 403308544 | bytes 1840128 | tf_op jit(solution)/shard_map/while/body/eval_jaxpr/dot_general | solution.py:42
  81.5 2.0 %fusion.46 = (f32[512]{0:T(512)S(1)}, f32[512,512]{1,0:T(8,128)S(1)}) fusion(f32[512,128]{1,0:T(8,128)S(1)} %get-tuple-element.336, f32[4,512,128]{2,1,0:T(8,128)} %get-tuple-element.335, s32[]{:T(128)} %get-tuple-element.321, pred[512]{0:T(512)(128)(4,1)S(1)} %dynamic-slice_reduce_fusion.5), kind=kOutput, calls=%fused_computation.55.clone.1 | convolution fusion | flops 403439104 | bytes 1575936 | tf_op jit(solution)/shard_map/while/body/eval_jaxpr/dot_general | solution.py:18
  83.5 0.2 fusion.47
  83.7 2.9 %convolution_add_fusion.4 = f32[512,128]{1,0:T(8,128)S(1)} fusion(f32[512,512]{1,0:T(8,128)S(1)} %get-tuple-element.267, f32[512]{0:T(512)S(1)} %max.10, pred[512]{0:T(512)(128)(4,1)S(1)} %dynamic-slice_reduce_fusion.5, f32[4,512,128]{2,1,0:T(8,128)} %get-tuple-element.337, s32[]{:T(128)} %get-tuple-element.321, ...), kind=kOutput, calls=%fused_computation.2.clone.1 | convolution fusion | flops 403308544 | bytes 1840128 | tf_op jit(solution)/shard_map/while/body/eval_jaxpr/dot_general | solution.py:42
  86.7 2.0 %fusion.46 = (f32[512]{0:T(512)S(1)}, f32[512,512]{1,0:T(8,128)S(1)}) fusion(f32[512,128]{1,0:T(8,128)S(1)} %get-tuple-element.336, f32[4,512,128]{2,1,0:T(8,128)} %get-tuple-element.335, s32[]{:T(128)} %get-tuple-element.321, pred[512]{0:T(512)(128)(4,1)S(1)} %dynamic-slice_reduce_fusion.5), kind=kOutput, calls=%fused_computation.55.clone.1 | convolution fusion | flops 403439104 | bytes 1575936 | tf_op jit(solution)/shard_map/while/body/eval_jaxpr/dot_general | solution.py:18
  88.7 0.2 fusion.47
  88.9 2.9 %convolution_add_fusion.4 = f32[512,128]{1,0:T(8,128)S(1)} fusion(f32[512,512]{1,0:T(8,128)S(1)} %get-tuple-element.267, f32[512]{0:T(512)S(1)} %max.10, pred[512]{0:T(512)(128)(4,1)S(1)} %dynamic-slice_reduce_fusion.5, f32[4,512,128]{2,1,0:T(8,128)} %get-tuple-element.337, s32[]{:T(128)} %get-tuple-element.321, ...), kind=kOutput, calls=%fused_computation.2.clone.1 | convolution fusion | flops 403308544 | bytes 1840128 | tf_op jit(solution)/shard_map/while/body/eval_jaxpr/dot_general | solution.py:42
  91.9 0.8 broadcast_divide_fusion
  (56 shorter events, 0.5 us)
Async XLA Ops:
  6.5 17.5 %copy-start = (s32[4,2,2]{0,2,1:T(2,128)S(1)}, s32[4,2,2]{0,2,1:T(2,128)}, u32[]{:S(2)}) copy-start(s32[4,2,2]{0,2,1:T(2,128)} %param.13) | copy-start | bytes 196
  6.5 13.9 %copy-start.2 = (f32[512,128]{1,0:T(8,128)S(1)}, f32[512,128]{1,0:T(8,128)}, u32[]{:S(2)}) copy-start(f32[512,128]{1,0:T(8,128)} %param.11) | copy-start | bytes 786436
  6.5 64.5 %all-gather.5.cloned.1.call-start = ((), (), s32[]{:S(2)}) async-start(), calls=%async_computation.1 | async-start | bytes 1310720 | tf_op jit(solution)/shard_map/all_gather | solution.py:97
  7.3 63.8 %all-gather.3.cloned.1.call-start = ((), (), s32[]{:S(2)}) async-start(), calls=%async_computation | async-start | bytes 1310720 | tf_op jit(solution)/shard_map/all_gather | solution.py:96
  7.3 20.7 %collective-permute-start = (f32[512,128]{1,0:T(8,128)}, f32[512,128]{1,0:T(8,128)S(1)}, u32[]{:S(2)}, u32[]{:S(2)}) collective-permute-start(f32[512,128]{1,0:T(8,128)} %param.10), channel_id=1, source_target_pairs={{0,4},{4,8},{8,12},{1,5},{5,9},{9,13},{2,6},{6,10},{10,14},{3,7},{... | collective-permute-start | bytes 786440 | tf_op jit(solution)/shard_map/ppermute | solution.py:14
  12.3 17.1 %collective-permute-start.1 = (f32[512,128]{1,0:T(8,128)}, f32[512,128]{1,0:T(8,128)S(1)}, u32[]{:S(2)}, u32[]{:S(2)}) collective-permute-start(f32[512,128]{1,0:T(8,128)} %param.10), channel_id=1, source_target_pairs={{4,0},{8,4},{12,8},{5,1},{9,5},{13,9},{6,2},{10,6},{14,10},{7,3},{... | collective-permute-start | bytes 786440 | tf_op jit(solution)/shard_map/ppermute | solution.py:14
  13.6 22.3 %collective-permute-start.2 = (f32[512,128]{1,0:T(8,128)}, f32[512,128]{1,0:T(8,128)S(1)}, u32[]{:S(2)}, u32[]{:S(2)}) collective-permute-start(f32[512,128]{1,0:T(8,128)} %param.10), channel_id=1, source_target_pairs={{0,8},{4,12},{1,9},{5,13},{2,10},{6,14},{3,11},{7,15},{16,24},{20,... | collective-permute-start | bytes 786440 | tf_op jit(solution)/shard_map/ppermute | solution.py:14
  19.1 18.2 %collective-permute-start.3 = (f32[512,128]{1,0:T(8,128)}, f32[512,128]{1,0:T(8,128)S(1)}, u32[]{:S(2)}, u32[]{:S(2)}) collective-permute-start(f32[512,128]{1,0:T(8,128)} %param.10), channel_id=1, source_target_pairs={{8,0},{12,4},{9,1},{13,5},{10,2},{14,6},{11,3},{15,7},{24,16},{28,... | collective-permute-start | bytes 786440 | tf_op jit(solution)/shard_map/ppermute | solution.py:14
  20.4 17.0 %collective-permute-start.4 = (f32[512,128]{1,0:T(8,128)S(1)}, f32[512,128]{1,0:T(8,128)S(1)}, u32[]{:S(2)}, u32[]{:S(2)}) collective-permute-start(f32[512,128]{1,0:T(8,128)S(1)} %copy-done.2), channel_id=1, source_target_pairs={{0,4},{4,8},{8,12},{1,5},{5,9},{9,13},{2,6},{6,10},{10,14},{3,7},{... | collective-permute-start | bytes 786440 | tf_op jit(solution)/shard_map/ppermute | solution.py:14
  28.1 13.0 %collective-permute-start.5 = (f32[512,128]{1,0:T(8,128)S(1)}, f32[512,128]{1,0:T(8,128)S(1)}, u32[]{:S(2)}, u32[]{:S(2)}) collective-permute-start(f32[512,128]{1,0:T(8,128)S(1)} %copy-done.2), channel_id=1, source_target_pairs={{4,0},{8,4},{12,8},{5,1},{9,5},{13,9},{6,2},{10,6},{14,10},{7,3},{... | collective-permute-start | bytes 786440 | tf_op jit(solution)/shard_map/ppermute | solution.py:14
  29.4 11.6 %collective-permute-start.6 = (f32[512,128]{1,0:T(8,128)S(1)}, f32[512,128]{1,0:T(8,128)S(1)}, u32[]{:S(2)}, u32[]{:S(2)}) collective-permute-start(f32[512,128]{1,0:T(8,128)S(1)} %copy-done.2), channel_id=1, source_target_pairs={{0,8},{4,12},{1,9},{5,13},{2,10},{6,14},{3,11},{7,15},{16,24},{20,... | collective-permute-start | bytes 786440 | tf_op jit(solution)/shard_map/ppermute | solution.py:14
  35.9 16.1 %collective-permute-start.7 = (f32[512,128]{1,0:T(8,128)S(1)}, f32[512,128]{1,0:T(8,128)}, u32[]{:S(2)}, u32[]{:S(2)}) collective-permute-start(f32[512,128]{1,0:T(8,128)S(1)} %copy-done.2), channel_id=1, source_target_pairs={{8,0},{12,4},{9,1},{13,5},{10,2},{14,6},{11,3},{15,7},{24,16},{28,... | collective-permute-start | bytes 786440 | tf_op jit(solution)/shard_map/ppermute | solution.py:14
  37.4 16.6 %copy-start.1 = (f32[512,128]{1,0:T(8,128)S(1)}, f32[512,128]{1,0:T(8,128)}, u32[]{:S(2)}) copy-start(f32[512,128]{1,0:T(8,128)} %param.9) | copy-start | bytes 786436
Sparse Core Ops, SparseCore 0:
  8.9 19.4 all-gather.4
  29.9 16.7 all-gather.2
where the time goes:
time: 100 us; the launch traced here: 99.5 us
  matrix products  35.4 us (35%)
  starting transfers between devices  25.7 us (26%)
  between operations  16 us (16%)
  waiting for transfers between devices  15.3 us (15%)
  other arithmetic  5.6 us (6%)
  local copies, waits for them, and re-layouts  1.14 us (1%)
    ppermute x8, starting transfers between devices, shifted(): return lax.ppermute(block, axis, route)  25.7 us
    dot_general x8, matrix products, absorb_block(): jnp.dot(weights, value_block, precision=lax.Precision.HIGHEST, preferred_...  23.2 us
    ppermute x8, waiting for transfers between devices, shifted(): return lax.ppermute(block, axis, route)  14.5 us
    dot_general x8, matrix products, score_block(): lax.dot_general(query_rows, key_rows, (((1,), (1,)), ((), ())), precision...  12.2 us
    concatenate x1, other arithmetic, per_device(): jnp.concatenate(far_values, axis=0)  2.02 us
  transfers between devices with their start and end apart: 10, of which 2 were waited for; matrix products, arithmetic and copies ran while one was open for 21% of the time, Pallas kernels for 0%

commit v1 on v0

v1 whole, which is shorter than its diff:
```python
import functools
import math

import jax
import jax.numpy as jnp
from jax import lax
from jax.experimental import pallas as pl
from jax.experimental.pallas import tpu as pltpu
from jax.sharding import PartitionSpec as P

masked_score = -1e30
MESH = pl.DeviceIdType.MESH


def pieces_of(block, count):
    pieces = []
    rest = block
    for index in range(count):
        piece = rest.astype(jnp.bfloat16)
        pieces.append(piece)
        if index + 1 < count:
            rest = rest - piece.astype(jnp.float32)
    return pieces


def kernel(
    blocks,
    groups,
    levels,
    chunks,
    q_hbm,
    k_hbm,
    v_hbm,
    mask_ref,
    flags_ref,
    out_ref,
    q_vmem,
    space_buf,
    frame_buf,
    query_parts,
    row_max,
    row_total,
    weighted,
    local_sem,
    space_send,
    space_recv,
    frame_send,
    frame_recv,
):
    rows, width = q_vmem.shape
    chunk_rows = rows // chunks
    depth = 2 ** (levels - 1)
    reach = blocks // 2
    chips = blocks // 2
    here = lax.axis_index("space")
    group = lax.axis_index("frame")

    partners = []
    for step in range(1, blocks):
        chip = lax.rem(here // 2 + step // 2, chips)
        core = lax.rem(here % 2 + step % 2, 2)
        other = chip * 2 + core
        distance = jnp.where(other > here, other - here, here - other)
        partners.append((other, distance <= reach))
    routes = [
        (0, group + 1, group + 1 < groups),
        (1, group - 1, group >= 1),
    ]

    local = [
        pltpu.make_async_copy(q_hbm, q_vmem, local_sem.at[0]),
        pltpu.make_async_copy(k_hbm, space_buf.at[here, 0], local_sem.at[1]),
        pltpu.make_async_copy(v_hbm, space_buf.at[here, 1], local_sem.at[2]),
    ]
    for copy in local:
        copy.start()

    barrier = pltpu.get_barrier_semaphore()
    expected = jnp.int32(0)
    for _, target, exists in routes:
        expected = expected + jnp.where(exists, 1, 0)

        @pl.when(exists)
        def _(target=target):
            pl.semaphore_signal(barrier, inc=1, device_id={"frame": target}, device_id_type=MESH)

    for other, near in partners:
        expected = expected + jnp.where(near, 1, 0)

        @pl.when(near)
        def _(other=other):
            pl.semaphore_signal(barrier, inc=1, device_id={"space": other}, device_id_type=MESH)

    pl.semaphore_wait(barrier, expected)

    def frame_copy(way, hop, chunk, part, target):
        span = pl.ds(chunk * chunk_rows, chunk_rows)
        if hop == 1:
            source = (k_hbm, v_hbm)[part].at[span]
        else:
            source = frame_buf.at[way, hop - 2, part, span]
        return pltpu.make_async_remote_copy(
            src_ref=source,
            dst_ref=frame_buf.at[way, hop - 1, part, span],
            send_sem=frame_send.at[way, hop - 1, chunk, part],
            recv_sem=frame_recv.at[way, hop - 1, chunk, part],
            device_id={"frame": target},
            device_id_type=MESH,
        )

    def space_copy(step, part, slot, target):
        return pltpu.make_async_remote_copy(
            src_ref=(k_hbm, v_hbm)[part],
            dst_ref=space_buf.at[slot, part],
            send_sem=space_send.at[step, part],
            recv_sem=space_recv.at[slot, part],
            device_id={"space": target},
            device_id_type=MESH,
        )

    for chunk in range(chunks):
        for way, target, exists in routes:

            @pl.when(exists)
            def _(way=way, target=target, chunk=chunk):
                for part in range(2):
                    frame_copy(way, 1, chunk, part, target).start()

    for step, (other, near) in enumerate(partners):

        @pl.when(near)
        def _(step=step, other=other):
            for part in range(2):
                space_copy(step, part, here, other).start()

    for copy in local:
        copy.wait()

    scale = math.log2(math.e) / math.sqrt(width)
    first, second, third = pieces_of(q_vmem[...] * scale, 3)
    query_parts[...] = jnp.concatenate([first, second, second, first, third, first], axis=1)
    row_max[...] = jnp.full_like(row_max, masked_score)
    row_total[...] = jnp.zeros_like(row_total)
    weighted[...] = jnp.zeros_like(weighted)

    def absorb(key_rows, value_rows, shift):
        k0, k1, k2 = pieces_of(key_rows, 3)
        scores = lax.dot_general(
            jnp.concatenate([k0, k1, k0, k1, k0, k2], axis=1),
            query_parts[...],
            (((1,), (1,)), ((), ())),
            preferred_element_type=jnp.float32,
        )
        old_max = row_max[...]
        new_max = jnp.maximum(old_max, jnp.max(scores, axis=0, keepdims=True) + shift)
        weights = jnp.exp2(scores - (new_max - shift))
        factor = jnp.exp2(old_max - new_max)
        row_max[...] = new_max
        row_total[...] = row_total[...] * factor + jnp.sum(weights, axis=0, keepdims=True)
        v_parts = jnp.concatenate(pieces_of(value_rows, 2), axis=1)
        w0, w1 = pieces_of(weights, 2)
        contract = (((0,), (0,)), ((), ()))
        product = lax.dot_general(v_parts, w0, contract, preferred_element_type=jnp.float32)
        product += lax.dot_general(v_parts, w1, contract, preferred_element_type=jnp.float32)
        weighted[...] = weighted[...] * factor + (product[:width] + product[width:])

    def absorb_space(slot, allowed):
        absorb(space_buf[slot, 0], space_buf[slot, 1], jnp.where(allowed > 0, 0.0, masked_score))

    def take_space(step):
        other, near = partners[step]

        @pl.when(near)
        def _():
            for part in range(2):
                space_copy(step, part, other, other).wait_recv()
            absorb_space(other, mask_ref[here, other])

    def take_frame(hop):
        for chunk in range(chunks):
            for way, target, exists in routes:
                arrives = (group >= hop) if way == 0 else (group + hop < groups)

                @pl.when(arrives)
                def _(way=way, chunk=chunk, target=target):
                    for part in range(2):
                        frame_copy(way, hop, chunk, part, target).wait_recv()

                if hop < depth:

                    @pl.when(arrives & exists)
                    def _(way=way, chunk=chunk, target=target):
                        for part in range(2):
                            frame_copy(way, hop + 1, chunk, part, target).start()

            if hop & (hop - 1):
                continue
            for way, _, _ in routes:
                arrives = (group >= hop) if way == 0 else (group + hop < groups)

                @pl.when(arrives)
                def _(way=way, chunk=chunk):
                    allowed = flags_ref[group, hop.bit_length() - 1, way]
                    span = pl.ds(chunk * chunk_rows, chunk_rows)
                    absorb(
                        frame_buf[way, hop - 1, 0, span],
                        frame_buf[way, hop - 1, 1, span],
                        jnp.where(allowed > 0, 0.0, masked_score),
                    )

    absorb_space(here, mask_ref[here, here])
    take_space(0)
    take_frame(1)
    for step in range(1, blocks - 1):
        take_space(step)
    for hop in range(2, depth + 1):
        take_frame(hop)

    out_ref[...] = (weighted[...] / row_total[...]).T

    for step, (other, near) in enumerate(partners):

        @pl.when(near)
        def _(step=step, other=other):
            for part in range(2):
                space_copy(step, part, here, other).wait_send()

    for hop in range(1, depth + 1):
        for way, target, exists in routes:
            origin = (group >= hop - 1) if way == 0 else (group + hop - 1 < groups)

            @pl.when(exists & origin)
            def _(way=way, hop=hop, target=target):
                for chunk in range(chunks):
                    for part in range(2):
                        frame_copy(way, hop, chunk, part, target).wait_send()


def per_device(queries, keys, values, block_mask, partner_flags):
    rows, width = queries.shape
    blocks = lax.axis_size("space")
    groups = lax.axis_size("frame")
    levels = partner_flags.shape[1]
    depth = 2 ** (levels - 1)
    chunks = 4
    any_space = pl.BlockSpec(memory_space=pl.ANY)
    scalar_space = pl.BlockSpec(memory_space=pltpu.SMEM)
    used = blocks + 2 * levels
    return pl.pallas_call(
        functools.partial(kernel, blocks, groups, levels, chunks),
        out_shape=jax.ShapeDtypeStruct((rows, width), jnp.float32),
        in_specs=[any_space] * 3 + [scalar_space] * 2,
        out_specs=pl.BlockSpec(memory_space=pltpu.VMEM),
        scratch_shapes=[
            pltpu.VMEM((rows, width), jnp.float32),
            pltpu.VMEM((blocks, 2, rows, width), jnp.float32),
            pltpu.VMEM((2, depth, 2, rows, width), jnp.float32),
            pltpu.VMEM((rows, 6 * width), jnp.bfloat16),
            pltpu.VMEM((1, rows), jnp.float32),
            pltpu.VMEM((1, rows), jnp.float32),
            pltpu.VMEM((width, rows), jnp.float32),
            pltpu.SemaphoreType.DMA((3,)),
            pltpu.SemaphoreType.DMA((blocks, 2)),
            pltpu.SemaphoreType.DMA((blocks, 2)),
            pltpu.SemaphoreType.DMA((2, depth, chunks, 2)),
            pltpu.SemaphoreType.DMA((2, depth, chunks, 2)),
        ],
        compiler_params=pltpu.CompilerParams(
            collective_id=0, has_side_effects=True, vmem_limit_bytes=48 * 2**20
        ),
        cost_estimate=pl.CostEstimate(
            flops=4 * used * rows * rows * width,
            bytes_accessed=16 * rows * width,
            transcendentals=used * rows * rows,
        ),
    )(queries, keys, values, block_mask, partner_flags)


def solution(mesh):
    split = P(("groups", "frame", "space"), None)
    return jax.shard_map(
        per_device,
        mesh=mesh,
        in_specs=(split, split, split, P(), P()),
        out_specs=split,
        check_vma=False,
    )
```

time: 100 us -> 35 us (0.35)
  matrix products: 35.4 us -> 0 us
  Pallas kernels: 0 us -> 30.4 us
  starting transfers between devices: 25.7 us -> 0 us
  between operations: 16 us -> 0.01 us
  waiting for transfers between devices: 15.3 us -> 0 us
  other arithmetic: 5.6 us -> 0 us
  local copies, waits for them, and re-layouts: 1.14 us -> 4.34 us
    dot_general x16 -> x0, matrix products: 35.4 us -> none  [the longest x8 23.2 us: absorb_block(): jnp.dot(weights, value_block, precision=lax.Precision.HIGHEST, preferred_...]
    pallas_call x0 -> x1, Pallas kernels: none -> 30.4 us  [per_device(): pl.pallas_call(functools.partial(kernel, blocks, groups, levels, chunks),...]
    ppermute x8 -> x0, starting transfers between devices: 25.7 us -> none  [shifted(): return lax.ppermute(block, axis, route)]
    ppermute x8 -> x0, waiting for transfers between devices: 14.5 us -> none  [shifted(): return lax.ppermute(block, axis, route)]
    unnamed x6 -> x10, local copies, waits for them, and re-layouts: 0.01 us -> 4.34 us
    concatenate x3 -> x0, other arithmetic: 2.1 us -> none  [the longest x1 2.02 us: per_device(): jnp.concatenate(far_values, axis=0)]
    reduce_sum x8 -> x0, other arithmetic: 1.69 us -> none  [absorb_block(): row_total = row_total * factor + jnp.sum(weights, axis=1)]
  transfers between devices with their start and end apart: 10 -> 0, of which waited for: 2 -> 0; matrix products, arithmetic and copies ran while one was open for 21% -> 0% of each run, Pallas kernels for 0% -> 0%
where the time goes in v1:
time: 35 us; the launch traced here: 34.8 us
  Pallas kernels  30.4 us (87%)
  local copies, waits for them, and re-layouts  4.34 us (12%)
    pallas_call x1, Pallas kernels, per_device(): pl.pallas_call(functools.partial(kernel, blocks, groups, levels, chunks),...  30.4 us
    unnamed x10, local copies, waits for them, and re-layouts  4.34 us

profile of v1, /device:TPU:0, one launch (start us, length us, event | category | flops | bytes accessed | tf_op | source)
XLA Modules:
  0.0 34.8 jit_solution(5292955558992212204)
XLA Ops:
  0.0 0.0 copy-start.3
  0.0 0.8 %copy.6.flags_ref = s32[4,2,2]{2,1,0:T(2,128)S(1)} copy(s32[4,2,2]{0,2,1:T(2,128)} %param.9) | data formatting | bytes 128 | tf_op args[4]
  0.8 0.0 copy-done.3
  0.8 0.0 copy-start
  0.8 0.9 %copy-done = f32[512,128]{1,0:T(8,128)S(1)} copy-done((f32[512,128]{1,0:T(8,128)S(1)}, f32[512,128]{1,0:T(8,128)}, u32[]{:S(2)}) %copy-start) | copy-done | bytes 262168
  1.7 0.0 copy-start.1
  1.7 0.9 %copy-done.1 = f32[512,128]{1,0:T(8,128)S(1)} copy-done((f32[512,128]{1,0:T(8,128)S(1)}, f32[512,128]{1,0:T(8,128)}, u32[]{:S(2)}) %copy-start.1) | copy-done | bytes 262168
  2.7 0.0 copy-start.2
  2.7 0.9 %copy-done.2 = f32[512,128]{1,0:T(8,128)S(1)} copy-done((f32[512,128]{1,0:T(8,128)S(1)}, f32[512,128]{1,0:T(8,128)}, u32[]{:S(2)}) %copy-start.2) | copy-done | bytes 262168
  3.6 30.4 %shard_map.55 = f32[512,128]{1,0:T(8,128)S(1)} custom-call(f32[512,128]{1,0:T(8,128)S(1)} %copy-done, f32[512,128]{1,0:T(8,128)S(1)} %copy-done.1, f32[512,128]{1,0:T(8,128)S(1)} %copy-done.2, s32[4,4]{1,0:T(4,128)S(1)} %copy-done.3, s32[4,2,2]{2,1,0:T(2,128)S(1)} %copy.6.flags_ref), custom_call_target="tpu_custom_call" | custom-call | flops 1073741824 | bytes 1048576 | tf_op jit(solution)/shard_map/pallas_call | solution.py:249
  34.1 0.7 %copy.8 = f32[512,128]{1,0:T(8,128)} copy(f32[512,128]{1,0:T(8,128)S(1)} %shard_map.55) | data formatting | bytes 524288
Async XLA Ops:
  0.0 0.8 %copy-start.3 = (s32[4,4]{1,0:T(4,128)S(1)}, s32[4,4]{1,0:T(4,128)}, u32[]{:S(2)}) copy-start(s32[4,4]{1,0:T(4,128)} %mask_ref.1) | copy-start | bytes 196
  0.8 1.0 %copy-start = (f32[512,128]{1,0:T(8,128)S(1)}, f32[512,128]{1,0:T(8,128)}, u32[]{:S(2)}) copy-start(f32[512,128]{1,0:T(8,128)} %q_hbm.1) | copy-start | bytes 786436
  1.7 0.9 %copy-start.1 = (f32[512,128]{1,0:T(8,128)S(1)}, f32[512,128]{1,0:T(8,128)}, u32[]{:S(2)}) copy-start(f32[512,128]{1,0:T(8,128)} %k_hbm.1) | copy-start | bytes 786436
  2.7 0.9 %copy-start.2 = (f32[512,128]{1,0:T(8,128)S(1)}, f32[512,128]{1,0:T(8,128)}, u32[]{:S(2)}) copy-start(f32[512,128]{1,0:T(8,128)} %v_hbm.1) | copy-start | bytes 786436

commit v2 on v1

--- a/solution.py
+++ b/solution.py
@@ -31,9 +31,11 @@
     q_hbm,
     k_hbm,
     v_hbm,
+    mask_hbm,
+    flags_hbm,
+    out_ref,
     mask_ref,
     flags_ref,
-    out_ref,
     q_vmem,
     space_buf,
     frame_buf,
@@ -71,9 +73,9 @@
         pltpu.make_async_copy(q_hbm, q_vmem, local_sem.at[0]),
         pltpu.make_async_copy(k_hbm, space_buf.at[here, 0], local_sem.at[1]),
         pltpu.make_async_copy(v_hbm, space_buf.at[here, 1], local_sem.at[2]),
+        pltpu.make_async_copy(mask_hbm, mask_ref, local_sem.at[3]),
+        pltpu.make_async_copy(flags_hbm, flags_ref, local_sem.at[4]),
     ]
-    for copy in local:
-        copy.start()
 
     barrier = pltpu.get_barrier_semaphore()
     expected = jnp.int32(0)
@@ -91,6 +93,8 @@
         def _(other=other):
             pl.semaphore_signal(barrier, inc=1, device_id={"space": other}, device_id_type=MESH)
 
+    for copy in local:
+        copy.start()
     pl.semaphore_wait(barrier, expected)
 
     def frame_copy(way, hop, chunk, part, target):
@@ -143,7 +147,7 @@
     row_total[...] = jnp.zeros_like(row_total)
     weighted[...] = jnp.zeros_like(weighted)
 
-    def absorb(key_rows, value_rows, shift):
+    def absorb(key_rows, read_values, shift):
         k0, k1, k2 = pieces_of(key_rows, 3)
         scores = lax.dot_general(
             jnp.concatenate([k0, k1, k0, k1, k0, k2], axis=1),
@@ -157,7 +161,7 @@
         factor = jnp.exp2(old_max - new_max)
         row_max[...] = new_max
         row_total[...] = row_total[...] * factor + jnp.sum(weights, axis=0, keepdims=True)
-        v_parts = jnp.concatenate(pieces_of(value_rows, 2), axis=1)
+        v_parts = jnp.concatenate(pieces_of(read_values(), 2), axis=1)
         w0, w1 = pieces_of(weights, 2)
         contract = (((0,), (0,)), ((), ()))
         product = lax.dot_general(v_parts, w0, contract, preferred_element_type=jnp.float32)
@@ -165,7 +169,7 @@
         weighted[...] = weighted[...] * factor + (product[:width] + product[width:])
 
     def absorb_space(slot, allowed):
-        absorb(space_buf[slot, 0], space_buf[slot, 1], jnp.where(allowed > 0, 0.0, masked_score))
+        absorb(space_buf[slot, 0], lambda: space_buf[slot, 1], jnp.where(allowed > 0, 0.0, masked_score))
 
     def take_space(step):
         other, near = partners[step]
@@ -176,37 +180,64 @@
                 space_copy(step, part, other, other).wait_recv()
             absorb_space(other, mask_ref[here, other])
 
+    def arrives(way, hop):
+        return (group >= hop) if way == 0 else (group + hop < groups)
+
     def take_frame(hop):
+        used = hop & (hop - 1) == 0
+        passed_on = hop < depth
+        lag = min(2, chunks - 1) if hop == 1 else 0
+
+        def pass_on(chunk):
+            for way, target, exists in routes:
+
+                @pl.when(arrives(way, hop) & exists)
+                def _(way=way, target=target):
+                    for part in range(2):
+                        frame_copy(way, hop + 1, chunk, part, target).start()
+
+        def attend(way, chunk, before_values):
+            allowed = flags_ref[hop.bit_length() - 1, way, group]
+            span = pl.ds(chunk * chunk_rows, chunk_rows)
+
+            def read_values():
+                before_values()
+                return frame_buf[way, hop - 1, 1, span]
+
+            absorb(
+                frame_buf[way, hop - 1, 0, span],
+                read_values,
+                jnp.where(allowed > 0, 0.0, masked_score),
+            )
+
         for chunk in range(chunks):
-            for way, target, exists in routes:
-                arrives = (group >= hop) if way == 0 else (group + hop < groups)
-
-                @pl.when(arrives)
-                def _(way=way, chunk=chunk, target=target):
-                    for part in range(2):
-                        frame_copy(way, hop, chunk, part, target).wait_recv()
-
-                if hop < depth:
-
-                    @pl.when(arrives & exists)
-                    def _(way=way, chunk=chunk, target=target):
-                        for part in range(2):
-                            frame_copy(way, hop + 1, chunk, part, target).start()
-
-            if hop & (hop - 1):
-                continue
-            for way, _, _ in routes:
-                arrives = (group >= hop) if way == 0 else (group + hop < groups)
-
-                @pl.when(arrives)
-                def _(way=way, chunk=chunk):
-                    allowed = flags_ref[group, hop.bit_length() - 1, way]
-                    span = pl.ds(chunk * chunk_rows, chunk_rows)
-                    absorb(
-                        frame_buf[way, hop - 1, 0, span],
-                        frame_buf[way, hop - 1, 1, span],
-                        jnp.where(allowed > 0, 0.0, masked_score),
-                    )
+            for way, target, _ in routes:
+                landed = [frame_copy(way, hop, chunk, part, target) for part in range(2)]
+                if used and not passed_on:
+
+                    @pl.when(arrives(way, hop))
+                    def _(way=way, landed=landed):
+                        landed[0].wait_recv()
+                        attend(way, chunk, landed[1].wait_recv)
+
+                else:
+
+                    @pl.when(arrives(way, hop))
+                    def _(landed=landed):
+                        for copy in landed:
+                            copy.wait_recv()
+
+            if passed_on and chunk >= lag:
+                pass_on(chunk - lag)
+                if chunk == chunks - 1:
+                    for late in range(chunks - lag, chunks):
+                        pass_on(late)
+            if used and passed_on:
+                for way, _, _ in routes:
+
+                    @pl.when(arrives(way, hop))
+                    def _(way=way):
+                        attend(way, chunk, lambda: None)
 
     absorb_space(here, mask_ref[here, here])
     take_space(0)
@@ -227,9 +258,8 @@
 
     for hop in range(1, depth + 1):
         for way, target, exists in routes:
-            origin = (group >= hop - 1) if way == 0 else (group + hop - 1 < groups)
-
-            @pl.when(exists & origin)
+
+            @pl.when(exists & arrives(way, hop - 1))
             def _(way=way, hop=hop, target=target):
                 for chunk in range(chunks):
                     for part in range(2):
@@ -243,15 +273,15 @@
     levels = partner_flags.shape[1]
     depth = 2 ** (levels - 1)
     chunks = 4
-    any_space = pl.BlockSpec(memory_space=pl.ANY)
-    scalar_space = pl.BlockSpec(memory_space=pltpu.SMEM)
     used = blocks + 2 * levels
     return pl.pallas_call(
         functools.partial(kernel, blocks, groups, levels, chunks),
         out_shape=jax.ShapeDtypeStruct((rows, width), jnp.float32),
-        in_specs=[any_space] * 3 + [scalar_space] * 2,
+        in_specs=[pl.BlockSpec(memory_space=pltpu.HBM)] * 5,
         out_specs=pl.BlockSpec(memory_space=pltpu.VMEM),
         scratch_shapes=[
+            pltpu.SMEM(block_mask.shape, jnp.int32),
+            pltpu.SMEM((levels, 2, groups), jnp.int32),
             pltpu.VMEM((rows, width), jnp.float32),
             pltpu.VMEM((blocks, 2, rows, width), jnp.float32),
             pltpu.VMEM((2, depth, 2, rows, width), jnp.float32),
@@ -259,7 +289,7 @@
             pltpu.VMEM((1, rows), jnp.float32),
             pltpu.VMEM((1, rows), jnp.float32),
             pltpu.VMEM((width, rows), jnp.float32),
-            pltpu.SemaphoreType.DMA((3,)),
+            pltpu.SemaphoreType.DMA((5,)),
             pltpu.SemaphoreType.DMA((blocks, 2)),
             pltpu.SemaphoreType.DMA((blocks, 2)),
             pltpu.SemaphoreType.DMA((2, depth, chunks, 2)),
@@ -273,7 +303,7 @@
             bytes_accessed=16 * rows * width,
             transcendentals=used * rows * rows,
         ),
-    )(queries, keys, values, block_mask, partner_flags)
+    )(queries, keys, values, block_mask, jnp.transpose(partner_flags, (1, 2, 0)))
 
 
 def solution(mesh):

time: 35 us -> 34.4 us (0.983)
  Pallas kernels: 30.4 us -> 29.2 us
  local copies, waits for them, and re-layouts: 4.34 us -> 4.92 us
    pallas_call x1, Pallas kernels: 30.4 us -> 29.2 us  [per_device(): pl.pallas_call(functools.partial(kernel, blocks, groups, levels, chunks),...]
    unnamed x10 -> x11, local copies, waits for them, and re-layouts: 4.34 us -> 4.92 us
where the time goes in v2:
time: 34.4 us; the launch traced here: 34.2 us
  Pallas kernels  29.2 us (85%)
  local copies, waits for them, and re-layouts  4.92 us (14%)
    pallas_call x1, Pallas kernels, per_device(): pl.pallas_call(functools.partial(kernel, blocks, groups, levels, chunks),...  29.2 us
    unnamed x11, local copies, waits for them, and re-layouts  4.92 us

profile of v2, /device:TPU:0, one launch (start us, length us, event | category | flops | bytes accessed | tf_op | source)
XLA Modules:
  0.0 34.2 jit_solution(10645918994355441780)
XLA Ops:
  0.0 0.0 copy-start
  0.0 0.9 %copy-done = f32[512,128]{1,0:T(8,128)S(1)} copy-done((f32[512,128]{1,0:T(8,128)S(1)}, f32[512,128]{1,0:T(8,128)}, u32[]{:S(2)}) %copy-start) | copy-done | bytes 262168
  1.0 0.0 copy-start.1
  1.0 0.9 %copy-done.1 = f32[512,128]{1,0:T(8,128)S(1)} copy-done((f32[512,128]{1,0:T(8,128)S(1)}, f32[512,128]{1,0:T(8,128)}, u32[]{:S(2)}) %copy-start.1) | copy-done | bytes 262168
  1.9 0.0 copy-start.2
  1.9 0.9 %copy-done.2 = f32[512,128]{1,0:T(8,128)S(1)} copy-done((f32[512,128]{1,0:T(8,128)S(1)}, f32[512,128]{1,0:T(8,128)}, u32[]{:S(2)}) %copy-start.2) | copy-done | bytes 262168
  2.9 0.0 copy-start.3
  2.9 0.7 %copy-done.3 = s32[4,4]{1,0:T(4,128)S(1)} copy-done((s32[4,4]{1,0:T(4,128)S(1)}, s32[4,4]{1,0:T(4,128)}, u32[]{:S(2)}) %copy-start.3) | copy-done | bytes 88
  3.5 0.0 copy-start.4
  3.5 0.7 %copy-done.4 = s32[4,2,2]{0,2,1:T(2,128)S(1)} copy-done((s32[4,2,2]{0,2,1:T(2,128)S(1)}, s32[4,2,2]{0,2,1:T(2,128)}, u32[]{:S(2)}) %copy-start.4) | copy-done | bytes 88
  4.2 29.2 %shard_map.55 = f32[512,128]{1,0:T(8,128)S(1)} custom-call(f32[512,128]{1,0:T(8,128)S(1)} %copy-done, f32[512,128]{1,0:T(8,128)S(1)} %copy-done.1, f32[512,128]{1,0:T(8,128)S(1)} %copy-done.2, s32[4,4]{1,0:T(4,128)S(1)} %copy-done.3, s32[2,2,4]{2,1,0:T(2,128)S(1)} %bitcast.1), custom_call_target="tpu_custom_call" | custom-call | flops 1073741824 | bytes 1048576 | tf_op jit(solution)/shard_map/pallas_call | solution.py:277
  33.5 0.7 %copy.7 = f32[512,128]{1,0:T(8,128)} copy(f32[512,128]{1,0:T(8,128)S(1)} %shard_map.55) | data formatting | bytes 524288
Async XLA Ops:
  0.0 0.9 %copy-start = (f32[512,128]{1,0:T(8,128)S(1)}, f32[512,128]{1,0:T(8,128)}, u32[]{:S(2)}) copy-start(f32[512,128]{1,0:T(8,128)} %q_hbm.1) | copy-start | bytes 786436
  1.0 0.9 %copy-start.1 = (f32[512,128]{1,0:T(8,128)S(1)}, f32[512,128]{1,0:T(8,128)}, u32[]{:S(2)}) copy-start(f32[512,128]{1,0:T(8,128)} %k_hbm.1) | copy-start | bytes 786436
  1.9 0.9 %copy-start.2 = (f32[512,128]{1,0:T(8,128)S(1)}, f32[512,128]{1,0:T(8,128)}, u32[]{:S(2)}) copy-start(f32[512,128]{1,0:T(8,128)} %v_hbm.1) | copy-start | bytes 786436
  2.9 0.7 %copy-start.3 = (s32[4,4]{1,0:T(4,128)S(1)}, s32[4,4]{1,0:T(4,128)}, u32[]{:S(2)}) copy-start(s32[4,4]{1,0:T(4,128)} %mask_hbm.1) | copy-start | bytes 196
  3.5 0.7 %copy-start.4 = (s32[4,2,2]{0,2,1:T(2,128)S(1)}, s32[4,2,2]{0,2,1:T(2,128)}, u32[]{:S(2)}) copy-start(s32[4,2,2]{0,2,1:T(2,128)} %param.9) | copy-start | bytes 196

commit v3 on v2

--- a/solution.py
+++ b/solution.py
@@ -296,7 +296,7 @@
             pltpu.SemaphoreType.DMA((2, depth, chunks, 2)),
         ],
         compiler_params=pltpu.CompilerParams(
-            collective_id=0, has_side_effects=True, vmem_limit_bytes=48 * 2**20
+            collective_id=0, has_side_effects=True, vmem_limit_bytes=60 * 2**20
         ),
         cost_estimate=pl.CostEstimate(
             flops=4 * used * rows * rows * width,

time: 34.4 us -> 32 us (0.930)
  local copies, waits for them, and re-layouts: 4.92 us -> 1.67 us
  Pallas kernels: 29.2 us -> 30.2 us
    unnamed x11 -> x1, local copies, waits for them, and re-layouts: 4.92 us -> 1.67 us
    pallas_call x1, Pallas kernels: 29.2 us -> 30.2 us  [per_device(): pl.pallas_call(functools.partial(kernel, blocks, groups, levels, chunks),...]
where the time goes in v3:
time: 32 us; the launch traced here: 31.9 us
  Pallas kernels  30.2 us (94%)
  local copies, waits for them, and re-layouts  1.67 us (5%)
    pallas_call x1, Pallas kernels, per_device(): pl.pallas_call(functools.partial(kernel, blocks, groups, levels, chunks),...  30.2 us
    unnamed x1, local copies, waits for them, and re-layouts  1.67 us

profile of v3, /device:TPU:0, one launch (start us, length us, event | category | flops | bytes accessed | tf_op | source)
XLA Modules:
  0.0 31.9 jit_solution(11133874996384672381)
XLA Ops:
  0.0 30.2 %shard_map.55 = f32[512,128]{1,0:T(8,128)} custom-call(f32[512,128]{1,0:T(8,128)} %q_hbm.1, f32[512,128]{1,0:T(8,128)} %k_hbm.1, f32[512,128]{1,0:T(8,128)} %v_hbm.1, s32[4,4]{1,0:T(4,128)} %mask_hbm.1, s32[2,2,4]{2,1,0:T(2,128)} %bitcast.1), custom_call_target="tpu_custom_call" | custom-call | flops 1073741824 | bytes 1048576 | tf_op jit(solution)/shard_map/pallas_call | solution.py:277
  30.2 1.7 %copy.7 = f32[512,128]{1,0:T(8,128)} copy(f32[512,128]{1,0:T(8,128)} %shard_map.55) | data formatting | bytes 524288

commit v4 on v2

--- a/solution.py
+++ b/solution.py
@@ -274,6 +274,10 @@
     depth = 2 ** (levels - 1)
     chunks = 4
     used = blocks + 2 * levels
+    arguments = [
+        pltpu.with_memory_space_constraint(argument, pltpu.HBM)
+        for argument in (queries, keys, values, block_mask, jnp.transpose(partner_flags, (1, 2, 0)))
+    ]
     return pl.pallas_call(
         functools.partial(kernel, blocks, groups, levels, chunks),
         out_shape=jax.ShapeDtypeStruct((rows, width), jnp.float32),
@@ -303,7 +307,7 @@
             bytes_accessed=16 * rows * width,
             transcendentals=used * rows * rows,
         ),
-    )(queries, keys, values, block_mask, jnp.transpose(partner_flags, (1, 2, 0)))
+    )(*arguments)
 
 
 def solution(mesh):

time: 34.4 us -> 30.4 us (0.88)
  local copies, waits for them, and re-layouts: 4.92 us -> 0.71 us
    unnamed x11 -> x1, local copies, waits for them, and re-layouts: 4.92 us -> 0.71 us
where the time goes in v4:
time: 30.4 us; the launch traced here: 30.2 us
  Pallas kernels  29.5 us (97%)
  local copies, waits for them, and re-layouts  0.71 us (2%)
    pallas_call x1, Pallas kernels, per_device(): pl.pallas_call(functools.partial(kernel, blocks, groups, levels, chunks),...  29.5 us
    unnamed x1, local copies, waits for them, and re-layouts  0.71 us

profile of v4, /device:TPU:0, one launch (start us, length us, event | category | flops | bytes accessed | tf_op | source)
XLA Modules:
  0.0 30.2 jit_solution(981953271668194500)
XLA Ops:
  0.0 29.5 %shard_map.55 = f32[512,128]{1,0:T(8,128)S(1)} custom-call(f32[512,128]{1,0:T(8,128)} %q_hbm.1, f32[512,128]{1,0:T(8,128)} %k_hbm.1, f32[512,128]{1,0:T(8,128)} %v_hbm.1, s32[4,4]{1,0:T(4,128)} %mask_hbm.1, s32[2,2,4]{2,1,0:T(2,128)} %bitcast.1), custom_call_target="tpu_custom_call" | custom-call | flops 1073741824 | bytes 1048576 | tf_op jit(solution)/shard_map/pallas_call | solution.py:281
  29.5 0.7 %copy.7 = f32[512,128]{1,0:T(8,128)} copy(f32[512,128]{1,0:T(8,128)S(1)} %shard_map.55) | data formatting | bytes 524288
